TPU v7x, 32 devices: a whole 2x2x4 slice. The times are simulated.
32 devices in a mesh: groups: 2 (over y), front: 4 (over z), batch: 2 (over x), line: 2 (over core).
Axes of the slice: x: 2, y: 2, z: 4, core: 2. Of those that a mesh axis runs over, the one named last changes fastest.
Arguments:
- injections: float32 [2048, 512], P('front', ('groups', 'batch')), parts along dimension 1, may hold values from -6 to 6
- switch_from: int32 [2, 512], P(None, ('groups', 'batch')), parts along dimension 1, may hold values from 0 to 2047
- switch_to: int32 [2, 512], P(None, ('groups', 'batch')), parts along dimension 1, may hold values from 0 to 2047
- switch_susc: float32 [2, 512], P(None, ('groups', 'batch')), parts along dimension 1, may hold values from 0.5 to 4
- coupling: float32 [2048, 512], P('front'), may hold values from -1 to 1
- pivot_inverse: float32 [2048, 512], P('front')
- branch_from: int32 [4096], P(('front', 'line')), may hold values from 0 to 2047, as said below
- branch_to: int32 [4096], P(('front', 'line')), may hold values from 0 to 2047, as said below
- branch_susc: float32 [4096], P(('front', 'line')), may hold values from 0.5 to 2
- branch_owner: int32 [4096, 1], P(('front', 'line')), may hold values from 0 to 7; in each aligned block of 512 rows (0 to 511, 512 to 1023, ...) at most 128 rows name the same one
- in_weight: float32 [128], replicated, may hold values from -4 to 4
- in_bias: float32 [128], replicated, may hold values from -1 to 1
- out_weight: bfloat16 [128, 128], replicated, may hold values from -0.5 to 0.5
Outputs:
- region_scores: bfloat16 [8, 512, 128], P(('front', 'line'), ('groups', 'batch')), parts along dimension 1
- angles: float32 [2048, 512], P('front', ('groups', 'batch')), parts along dimension 1
There are 2 independent parts, one for each index of `groups`. A program takes and returns all parts, laid end to end along the dimension named above; an argument that names none is the same for every part. Nothing has to cross between parts.
Inputs may be any that keep to these rules, and one draw needn't show every extreme that they name: `branch_from`: the bus of row r lies in slab s = r // 1024, between s * 512 and s * 512 + 511. `branch_to`: the bus of row r lies in slab s = r // 1024 or in slab s + 1. `branch_owner`: in each aligned block of 512 rows (the branches of one device) no owner is named by more than 128 rows.
All inputs are finite; a program needn't handle non-finite values.
Results may differ from a plain program's by a relative error of at most 0.005.
Values sent between devices are 32-bit elements; how exact they have to be, the bound alone decides.
A program may use at most 64 MiB of HBM per device.

v0:
```python
import jax
import jax.numpy as jnp
from jax import lax
from jax.sharding import PartitionSpec as P

K = 2
BR_DEV = 512


def from_behind(value, axis, by):
    count = lax.axis_size(axis)
    pairs = [(i, i + by) for i in range(count) if 0 <= i + by < count]
    return lax.ppermute(value, axis, pairs)


def product(operand, against):
    return jnp.dot(
        operand, against, precision=lax.Precision.HIGHEST, preferred_element_type=jnp.float32
    )


def centered_tanh(loadings, in_weight, in_bias):
    return jnp.tanh(loadings[..., None] * in_weight + in_bias) - jnp.tanh(in_bias)


def capacitance_solve(terms, switch_susc):
    switches = switch_susc.shape[0]
    factor = [[None] * switches for row_at in range(switches)]
    for row_at in range(switches):
        for col_at in range(row_at + 1):
            partial_sum = terms[row_at, 1 + col_at]
            if row_at == col_at:
                partial_sum = partial_sum + 1.0 / switch_susc[row_at]
            for inner_at in range(col_at):
                partial_sum = partial_sum - factor[row_at][inner_at] * factor[col_at][inner_at]
            if row_at == col_at:
                factor[row_at][col_at] = jnp.sqrt(partial_sum)
            else:
                factor[row_at][col_at] = partial_sum / factor[col_at][col_at]
    lower_part = []
    for row_at in range(switches):
        running = terms[row_at, 0]
        for inner_at in range(row_at):
            running = running - factor[row_at][inner_at] * lower_part[inner_at]
        lower_part.append(running / factor[row_at][row_at])
    weights = [None] * switches
    for row_at in reversed(range(switches)):
        running = lower_part[row_at]
        for inner_at in range(row_at + 1, switches):
            running = running - factor[inner_at][row_at] * weights[inner_at]
        weights[row_at] = running / factor[row_at][row_at]
    return jnp.stack(weights)


def body(
    injections,
    switch_from,
    switch_to,
    switch_susc,
    coupling,
    pivot_inverse,
    branch_from,
    branch_to,
    branch_susc,
    branch_owner,
    in_weight,
    in_bias,
    out_weight,
):
    fronts = lax.axis_size("front")
    front_at = lax.axis_index("front")
    slab_size = coupling.shape[1]
    topo_count = injections.shape[1]
    first_bus = front_at * slab_size
    bus_ids = first_bus + jnp.arange(slab_size, dtype=jnp.int32)
    from_hot = (bus_ids[:, None, None] == switch_from[None]).astype(jnp.float32)
    to_hot = (bus_ids[:, None, None] == switch_to[None]).astype(jnp.float32)
    incidence = from_hot - to_hot
    stacked = jnp.concatenate([injections[:, None, :], incidence], axis=1).reshape(slab_size, -1)

    def lower_step(step_at, current):
        arrived = from_behind(current, "front", 1)
        return stacked - product(coupling, arrived)

    lowered = lax.fori_loop(0, fronts - 1, lower_step, stacked)
    pivoted = product(pivot_inverse, lowered)

    def upper_step(step_at, current):
        arrived = from_behind(product(coupling.T, current), "front", -1)
        return pivoted - arrived

    solved = lax.fori_loop(0, fronts - 1, upper_step, pivoted)
    solved_cols = solved.reshape(slab_size, K + 1, topo_count)
    local_terms = jnp.einsum(
        "bit,bct->ict", incidence, solved_cols, precision=lax.Precision.HIGHEST
    )
    terms = lax.psum(local_terms, "front")
    weights = capacitance_solve(terms, switch_susc)
    angles = solved_cols[:, 0, :] - jnp.einsum(
        "bit,it->bt", solved_cols[:, 1:, :], weights, precision=lax.Precision.HIGHEST
    )
    following = from_behind(angles, "front", -1)
    joined = jnp.concatenate([angles, following], axis=0)
    flows = branch_susc[:, None] * (joined[branch_from - first_bus] - joined[branch_to - first_bus])
    owners = lax.axis_size(("front", "line"))
    capacity = 2 * BR_DEV // owners
    owner_ids = branch_owner[:, 0]
    owner_hot = (owner_ids[:, None] == jnp.arange(owners, dtype=jnp.int32)[None]).astype(jnp.int32)
    before = jnp.cumsum(owner_hot, axis=0) - owner_hot
    position = jnp.sum(before * owner_hot, axis=1)
    slot_ids = owner_ids * capacity + position
    dispatch = (jnp.arange(owners * capacity, dtype=jnp.int32)[:, None] == slot_ids[None]).astype(
        jnp.float32
    )
    outgoing = product(dispatch, flows).reshape(owners, capacity, topo_count)
    arrived = lax.all_to_all(outgoing, ("front", "line"), split_axis=0, concat_axis=0, tiled=True)
    slot_rows = arrived.reshape(-1, arrived.shape[2])
    span_size = 32
    blocks = slot_rows.reshape(-1, span_size, slot_rows.shape[1])

    def accumulate(running, slot_block):
        return (running + jnp.sum(centered_tanh(slot_block, in_weight, in_bias), axis=0), None)

    start_sum = jnp.zeros((slot_rows.shape[1], in_weight.shape[0]), jnp.float32)
    summed, unused = lax.scan(accumulate, start_sum, blocks)
    pooled = (summed * BR_DEV ** (-0.5)).astype(jnp.bfloat16)
    region_scores = jnp.dot(pooled, out_weight, preferred_element_type=jnp.float32).astype(
        jnp.bfloat16
    )
    return (region_scores[None], angles)


def solution(mesh):
    in_specs = (
        P("front", ("groups", "batch")),
        P(None, ("groups", "batch")),
        P(None, ("groups", "batch")),
        P(None, ("groups", "batch")),
        P("front", None),
        P("front", None),
        P(("front", "line")),
        P(("front", "line")),
        P(("front", "line")),
        P(("front", "line"), None),
        P(),
        P(),
        P(),
    )
    out_specs = (P(("front", "line"), ("groups", "batch"), None), P("front", ("groups", "batch")))
    return jax.shard_map(body, mesh=mesh, in_specs=in_specs, out_specs=out_specs, check_vma=False)
```

profile of v0, /device:TPU:0, one launch (start us, length us, event | category | flops | bytes accessed | tf_op | source)
XLA Modules:
  0.0 243.3 jit_solution(18174583019754320143)
XLA Ops:
  4.5 73.9 %while.32 = (s32[]{:T(128)}, f32[512,384]{1,0:T(8,128)}, f32[512,512]{1,0:T(8,128)S(1)}, f32[512,384]{1,0:T(8,128)S(1)}, s32[]{:T(128)}) while((s32[]{:T(128)}, f32[512,384]{1,0:T(8,128)}, f32[512,512]{1,0:T(8,128)S(1)}, f32[512,384]{1,0:T(8,128)S(1)}, s32[]{:T(128)}) %tuple.77), condition=%wide.region_4.0_spmd, body=%wide.region_3.0_spmd.sunk | while | flops 1208156160 | bytes 6553701 | solution.py:85
  4.5 5.8 %collective-permute-start = (f32[512,384]{1,0:T(8,128)}, f32[512,384]{1,0:T(8,128)}, u32[]{:S(2)}, u32[]{:S(2)}) collective-permute-start(f32[512,384]{1,0:T(8,128)} %get-tuple-element.274), channel_id=1, source_target_pairs={{0,4},{4,8},{8,12},{1,5},{5,9},{9,13},{2,6},{6,10},{10,14},{3,7},{... | collective-permute-start | bytes 2359304 | tf_op jit(solution)/shard_map/while/body/eval_jaxpr/ppermute | solution.py:13
  10.3 16.2 %collective-permute-done = f32[512,384]{1,0:T(8,128)} collective-permute-done((f32[512,384]{1,0:T(8,128)}, f32[512,384]{1,0:T(8,128)}, u32[]{:S(2)}, u32[]{:S(2)}) %collective-permute-start) | collective-permute-done | bytes 786464 | tf_op jit(solution)/shard_map/while/body/eval_jaxpr/ppermute | solution.py:13
  26.6 3.8 %convolution_subtract_fusion.2 = f32[512,384]{1,0:T(8,128)} fusion(f32[512,384]{1,0:T(8,128)S(1)} %get-tuple-element.281, f32[512,512]{1,0:T(8,128)S(1)} %get-tuple-element.280, f32[512,384]{1,0:T(8,128)} %collective-permute-done), kind=kOutput, calls=%fused_computation.2.clone.1 | convolution fusion | flops 1208156160 | bytes 3407872 | tf_op jit(solution)/shard_map/while/body/eval_jaxpr/dot_general | solution.py:17
  30.4 5.3 %collective-permute-start = (f32[512,384]{1,0:T(8,128)}, f32[512,384]{1,0:T(8,128)}, u32[]{:S(2)}, u32[]{:S(2)}) collective-permute-start(f32[512,384]{1,0:T(8,128)} %get-tuple-element.274), channel_id=1, source_target_pairs={{0,4},{4,8},{8,12},{1,5},{5,9},{9,13},{2,6},{6,10},{10,14},{3,7},{... | collective-permute-start | bytes 2359304 | tf_op jit(solution)/shard_map/while/body/eval_jaxpr/ppermute | solution.py:13
  35.7 15.4 %collective-permute-done = f32[512,384]{1,0:T(8,128)} collective-permute-done((f32[512,384]{1,0:T(8,128)}, f32[512,384]{1,0:T(8,128)}, u32[]{:S(2)}, u32[]{:S(2)}) %collective-permute-start) | collective-permute-done | bytes 786464 | tf_op jit(solution)/shard_map/while/body/eval_jaxpr/ppermute | solution.py:13
  51.0 3.8 %convolution_subtract_fusion.2 = f32[512,384]{1,0:T(8,128)} fusion(f32[512,384]{1,0:T(8,128)S(1)} %get-tuple-element.281, f32[512,512]{1,0:T(8,128)S(1)} %get-tuple-element.280, f32[512,384]{1,0:T(8,128)} %collective-permute-done), kind=kOutput, calls=%fused_computation.2.clone.1 | convolution fusion | flops 1208156160 | bytes 3407872 | tf_op jit(solution)/shard_map/while/body/eval_jaxpr/dot_general | solution.py:17
  54.9 5.3 %collective-permute-start = (f32[512,384]{1,0:T(8,128)}, f32[512,384]{1,0:T(8,128)}, u32[]{:S(2)}, u32[]{:S(2)}) collective-permute-start(f32[512,384]{1,0:T(8,128)} %get-tuple-element.274), channel_id=1, source_target_pairs={{0,4},{4,8},{8,12},{1,5},{5,9},{9,13},{2,6},{6,10},{10,14},{3,7},{... | collective-permute-start | bytes 2359304 | tf_op jit(solution)/shard_map/while/body/eval_jaxpr/ppermute | solution.py:13
  60.1 14.4 %collective-permute-done = f32[512,384]{1,0:T(8,128)} collective-permute-done((f32[512,384]{1,0:T(8,128)}, f32[512,384]{1,0:T(8,128)}, u32[]{:S(2)}, u32[]{:S(2)}) %collective-permute-start) | collective-permute-done | bytes 786464 | tf_op jit(solution)/shard_map/while/body/eval_jaxpr/ppermute | solution.py:13
  74.5 3.8 %convolution_subtract_fusion.2 = f32[512,384]{1,0:T(8,128)} fusion(f32[512,384]{1,0:T(8,128)S(1)} %get-tuple-element.281, f32[512,512]{1,0:T(8,128)S(1)} %get-tuple-element.280, f32[512,384]{1,0:T(8,128)} %collective-permute-done), kind=kOutput, calls=%fused_computation.2.clone.1 | convolution fusion | flops 1208156160 | bytes 3407872 | tf_op jit(solution)/shard_map/while/body/eval_jaxpr/dot_general | solution.py:17
  78.4 4.7 %convolution_bitcast_fusion = f32[512,384]{0,1:T(8,128)} fusion(f32[512,384]{1,0:T(8,128)} %get-tuple-element.98, f32[512,512]{1,0:T(8,128)S(1)} %copy-done), kind=kOutput, calls=%fused_computation.8 | convolution fusion | flops 1207959552 | bytes 2621440 | tf_op jit(solution)/shard_map/dot_general | solution.py:17
  83.1 1.4 copy.34
  85.4 72.7 %while.33 = (s32[]{:T(128)}, f32[512,384]{1,0:T(8,128)}, f32[512,512]{1,0:T(8,128)S(1)}, f32[512,384]{1,0:T(8,128)S(1)}, s32[]{:T(128)}) while((s32[]{:T(128)}, f32[512,384]{1,0:T(8,128)}, f32[512,512]{1,0:T(8,128)S(1)}, f32[512,384]{1,0:T(8,128)S(1)}, s32[]{:T(128)}) %tuple.78), condition=%wide.region_6.7_spmd, body=%wide.region_5.0_spmd.sunk | while | flops 1208156160 | bytes 8126565 | solution.py:92
  85.4 3.8 %fusion.37 = f32[512,384]{1,0:T(8,128)} fusion(f32[512,512]{1,0:T(8,128)S(1)} %get-tuple-element.295, f32[512,384]{1,0:T(8,128)} %get-tuple-element.289), kind=kOutput, calls=%fused_computation.57.clone.1 | convolution fusion | flops 1207959552 | bytes 2621440 | tf_op jit(solution)/shard_map/while/body/eval_jaxpr/dot_general | solution.py:17
  90.5 18.2 %collective-permute-done.1 = f32[512,384]{1,0:T(8,128)} collective-permute-done((f32[512,384]{1,0:T(8,128)}, f32[512,384]{1,0:T(8,128)}, u32[]{:S(2)}, u32[]{:S(2)}) %collective-permute-start.1) | collective-permute-done | bytes 786464 | tf_op jit(solution)/shard_map/while/body/eval_jaxpr/ppermute | solution.py:13
  108.7 2.1 sub.95
  110.8 3.8 %fusion.37 = f32[512,384]{1,0:T(8,128)} fusion(f32[512,512]{1,0:T(8,128)S(1)} %get-tuple-element.295, f32[512,384]{1,0:T(8,128)} %get-tuple-element.289), kind=kOutput, calls=%fused_computation.57.clone.1 | convolution fusion | flops 1207959552 | bytes 2621440 | tf_op jit(solution)/shard_map/while/body/eval_jaxpr/dot_general | solution.py:17
  116.0 16.8 %collective-permute-done.1 = f32[512,384]{1,0:T(8,128)} collective-permute-done((f32[512,384]{1,0:T(8,128)}, f32[512,384]{1,0:T(8,128)}, u32[]{:S(2)}, u32[]{:S(2)}) %collective-permute-start.1) | collective-permute-done | bytes 786464 | tf_op jit(solution)/shard_map/while/body/eval_jaxpr/ppermute | solution.py:13
  132.8 2.1 sub.95
  134.9 3.8 %fusion.37 = f32[512,384]{1,0:T(8,128)} fusion(f32[512,512]{1,0:T(8,128)S(1)} %get-tuple-element.295, f32[512,384]{1,0:T(8,128)} %get-tuple-element.289), kind=kOutput, calls=%fused_computation.57.clone.1 | convolution fusion | flops 1207959552 | bytes 2621440 | tf_op jit(solution)/shard_map/while/body/eval_jaxpr/dot_general | solution.py:17
  140.0 15.9 %collective-permute-done.1 = f32[512,384]{1,0:T(8,128)} collective-permute-done((f32[512,384]{1,0:T(8,128)}, f32[512,384]{1,0:T(8,128)}, u32[]{:S(2)}, u32[]{:S(2)}) %collective-permute-start.1) | collective-permute-done | bytes 786464 | tf_op jit(solution)/shard_map/while/body/eval_jaxpr/ppermute | solution.py:13
  155.9 2.1 sub.95
  158.0 1.4 copy.36
  159.4 4.5 %convolution_bitcast_fusion.1 = f32[2,3,128]{1,0,2:T(2,128)S(1)} fusion(f32[512,3,128]{0,2,1:T(8,128)S(1)} %bitcast.81, f32[512,2,128]{0,2,1:T(8,128)S(1)} %convert_subtract_fusion), kind=kOutput, calls=%fused_computation.9 | convolution fusion | flops 4718592 | bytes 1313792 | tf_op jit(solution)/shard_map/bit,bct->ict/dot_general | solution.py:94
  163.9 19.6 %psum.7 = f32[2,3,128]{1,0,2:T(2,128)S(1)} all-reduce(f32[2,3,128]{1,0,2:T(2,128)S(1)} %convolution_bitcast_fusion.1), channel_id=1, replica_groups=mesh['groups'=2,'front'=4,'batch'=2,'line'=2] {'front'}, use_global_device_ids=true, to_apply=%region_7.8 | all-reduce | flops 768 | bytes 6144 | tf_op jit(solution)/shard_map/psum | solution.py:97
  183.5 2.2 slice_reduce_fusion.2
  186.2 1.3 collective-permute-start.2
  189.1 5.4 %collective-permute-done.2 = f32[512,128]{1,0:T(8,128)S(1)} collective-permute-done((f32[512,128]{1,0:T(8,128)S(1)}, f32[512,128]{1,0:T(8,128)S(1)}, u32[]{:S(2)}, u32[]{:S(2)}) %collective-permute-start.2) | collective-permute-done | bytes 262176 | tf_op jit(solution)/shard_map/ppermute | solution.py:13
  196.7 1.9 fusion
  198.6 3.5 %all-to-all-start = ((f32[8,128,128]{2,1,0:T(8,128)}), f32[8,128,128]{2,1,0:T(8,128)S(1)}, u32[]{:S(2)}, u32[]{:S(2)}) async-start(f32[8,128,128]{2,1,0:T(8,128)} %bitcast.13), calls=%async_computation | async-start | bytes 1048576 | tf_op jit(solution)/shard_map/all_to_all | solution.py:116
  202.1 15.2 %all-to-all-done = f32[8,128,128]{2,1,0:T(8,128)S(1)} async-done(((f32[8,128,128]{2,1,0:T(8,128)}), f32[8,128,128]{2,1,0:T(8,128)S(1)}, u32[]{:S(2)}, u32[]{:S(2)}) %all-to-all-start) | async-done | bytes 524320 | tf_op jit(solution)/shard_map/all_to_all | solution.py:116
  217.4 25.2 %while.34 = (s32[]{:T(128)}, f32[128,128]{1,0:T(8,128)S(1)}, f32[32,32,128]{2,1,0:T(8,128)S(1)}, f32[128]{0:T(128)S(1)}, f32[128]{0:T(128)S(1)}, /*index=5*/f32[1,1,128]{2,1,0:T(1,128)S(1)}, s32[]{:T(128)}, s32[]{:T(128)}) while((s32[]{:T(128)}, f32[128,128]{1,0:T(8,128)S(1)}, f32[32,32,128]{2,1,0:T(8,128)S(1)}, ...), condition=%wide.region_10.11_spmd.clone, body=%wide.region_8.10_spmd.clone.sunk | while | flops 2113539 | bytes 312931 | solution.py:125
  (152 shorter events, 37.3 us)
Async XLA Ops:
  0.6 77.8 %copy-start = (f32[512,512]{1,0:T(8,128)S(1)}, f32[512,512]{1,0:T(8,128)}, u32[]{:S(2)}) copy-start(f32[512,512]{1,0:T(8,128)} %param.24) | copy-start | bytes 3145732
  3.0 1.5 copy-start.1
  4.5 22.0 %collective-permute-start = (f32[512,384]{1,0:T(8,128)}, f32[512,384]{1,0:T(8,128)}, u32[]{:S(2)}, u32[]{:S(2)}) collective-permute-start(f32[512,384]{1,0:T(8,128)} %get-tuple-element.274), channel_id=1, source_target_pairs={{0,4},{4,8},{8,12},{1,5},{5,9},{9,13},{2,6},{6,10},{10,14},{3,7},{... | collective-permute-start | bytes 2359304 | tf_op jit(solution)/shard_map/while/body/eval_jaxpr/ppermute | solution.py:13
  30.4 20.6 %collective-permute-start = (f32[512,384]{1,0:T(8,128)}, f32[512,384]{1,0:T(8,128)}, u32[]{:S(2)}, u32[]{:S(2)}) collective-permute-start(f32[512,384]{1,0:T(8,128)} %get-tuple-element.274), channel_id=1, source_target_pairs={{0,4},{4,8},{8,12},{1,5},{5,9},{9,13},{2,6},{6,10},{10,14},{3,7},{... | collective-permute-start | bytes 2359304 | tf_op jit(solution)/shard_map/while/body/eval_jaxpr/ppermute | solution.py:13
  54.9 19.7 %collective-permute-start = (f32[512,384]{1,0:T(8,128)}, f32[512,384]{1,0:T(8,128)}, u32[]{:S(2)}, u32[]{:S(2)}) collective-permute-start(f32[512,384]{1,0:T(8,128)} %get-tuple-element.274), channel_id=1, source_target_pairs={{0,4},{4,8},{8,12},{1,5},{5,9},{9,13},{2,6},{6,10},{10,14},{3,7},{... | collective-permute-start | bytes 2359304 | tf_op jit(solution)/shard_map/while/body/eval_jaxpr/ppermute | solution.py:13
  89.2 19.5 %collective-permute-start.1 = (f32[512,384]{1,0:T(8,128)}, f32[512,384]{1,0:T(8,128)}, u32[]{:S(2)}, u32[]{:S(2)}) collective-permute-start(f32[512,384]{1,0:T(8,128)} %fusion.37), channel_id=1, source_target_pairs={{4,0},{8,4},{12,8},{5,1},{9,5},{13,9},{6,2},{10,6},{14,10},{7,3},{... | collective-permute-start | bytes 2359304 | tf_op jit(solution)/shard_map/while/body/eval_jaxpr/ppermute | solution.py:13
  114.7 18.1 %collective-permute-start.1 = (f32[512,384]{1,0:T(8,128)}, f32[512,384]{1,0:T(8,128)}, u32[]{:S(2)}, u32[]{:S(2)}) collective-permute-start(f32[512,384]{1,0:T(8,128)} %fusion.37), channel_id=1, source_target_pairs={{4,0},{8,4},{12,8},{5,1},{9,5},{13,9},{6,2},{10,6},{14,10},{7,3},{... | collective-permute-start | bytes 2359304 | tf_op jit(solution)/shard_map/while/body/eval_jaxpr/ppermute | solution.py:13
  138.7 17.2 %collective-permute-start.1 = (f32[512,384]{1,0:T(8,128)}, f32[512,384]{1,0:T(8,128)}, u32[]{:S(2)}, u32[]{:S(2)}) collective-permute-start(f32[512,384]{1,0:T(8,128)} %fusion.37), channel_id=1, source_target_pairs={{4,0},{8,4},{12,8},{5,1},{9,5},{13,9},{6,2},{10,6},{14,10},{7,3},{... | collective-permute-start | bytes 2359304 | tf_op jit(solution)/shard_map/while/body/eval_jaxpr/ppermute | solution.py:13
  163.9 21.8 %copy-start.8 = (f32[2,128]{1,0:T(2,128)S(1)}, f32[2,128]{1,0:T(2,128)}, u32[]{:S(2)}) copy-start(f32[2,128]{1,0:T(2,128)} %param.22) | copy-start | bytes 3076
  185.9 1.7 copy-start.6
  185.9 1.7 copy-start.7
  185.9 1.7 copy-start.4
  186.2 9.4 %copy-start.2 = (f32[512,128]{1,0:T(8,128)}, f32[512,128]{1,0:T(8,128)S(1)}, u32[]{:S(2)}) copy-start(f32[512,128]{1,0:T(8,128)S(1)} %bitcast_subtract_fusion) | copy-start | bytes 786436
  186.2 8.3 %collective-permute-start.2 = (f32[512,128]{1,0:T(8,128)S(1)}, f32[512,128]{1,0:T(8,128)S(1)}, u32[]{:S(2)}, u32[]{:S(2)}) collective-permute-start(f32[512,128]{1,0:T(8,128)S(1)} %bitcast_subtract_fusion), channel_id=1, source_target_pairs={{4,0},{8,4},{12,8},{5,1},{9,5},{13,9},{6,2},{10,6},{14,10},{7,3},{... | collective-permute-start | bytes 786440 | tf_op jit(solution)/shard_map/ppermute | solution.py:13
  195.6 1.1 copy-start.5
  196.7 5.5 %copy-start.10 = (f32[128]{0:T(128)S(1)}, f32[128]{0:T(128)}, u32[]{:S(2)}) copy-start(f32[128]{0:T(128)} %param.30) | copy-start | bytes 1540
  196.7 20.7 %copy-start.9 = (f32[128]{0:T(128)S(1)}, f32[128]{0:T(128)}, u32[]{:S(2)}) copy-start(f32[128]{0:T(128)} %param.29) | copy-start | bytes 1540
  198.6 18.8 %all-to-all-start = ((f32[8,128,128]{2,1,0:T(8,128)}), f32[8,128,128]{2,1,0:T(8,128)S(1)}, u32[]{:S(2)}, u32[]{:S(2)}) async-start(f32[8,128,128]{2,1,0:T(8,128)} %bitcast.13), calls=%async_computation | async-start | bytes 1048576 | tf_op jit(solution)/shard_map/all_to_all | solution.py:116
  217.4 25.2 %copy-start.3 = (bf16[128,128]{1,0:T(8,128)(2,1)S(1)}, bf16[128,128]{1,0:T(8,128)(2,1)}, u32[]{:S(2)}) copy-start(bf16[128,128]{1,0:T(8,128)(2,1)} %param.31) | copy-start | bytes 98308
where the time goes:
time: 244 us; the launch traced here: 243 us
  waiting for transfers between devices  118 us (48%)
  matrix products  34.9 us (14%)
  other arithmetic  32.3 us (13%)
  starting transfers between devices  24.9 us (10%)
  blocking collectives  19.6 us (8%)
  local copies, waits for them, and re-layouts  11.7 us (5%)
    ppermute x7, waiting for transfers between devices, from_behind(): return lax.ppermute(value, axis, pairs)  102 us
    dot_general x8, matrix products, product(): jnp.dot(operand, against, precision=lax.Precision.HIGHEST, preferred_elem...  29.7 us
    reduce_sum x32, other arithmetic, accumulate(): jnp.sum(centered_tanh(slot_block, in_weight, in_bias), axis=0)  23 us
    ppermute x7, starting transfers between devices, from_behind(): return lax.ppermute(value, axis, pairs)  21.5 us
    psum x1, blocking collectives, body(): terms = lax.psum(local_terms, 'front')  19.6 us
    all_to_all x1, waiting for transfers between devices, body(): lax.all_to_all(outgoing, ('front', 'line'), split_axis=0, concat_axis=0,...  15.2 us
    sub x3, other arithmetic, upper_step(): return pivoted - arrived  6.31 us
  transfers between devices with their start and end apart: 8, of which 8 were waited for; matrix products, arithmetic and copies ran while one was open for 1% of the time, Pallas kernels for 0%

commit v1 on v0

--- a/solution.py
+++ b/solution.py
@@ -94,7 +94,7 @@
     local_terms = jnp.einsum(
         "bit,bct->ict", incidence, solved_cols, precision=lax.Precision.HIGHEST
     )
-    terms = lax.psum(local_terms, "front")
+    terms = jnp.sum(lax.all_gather(local_terms, "front"), axis=0)
     weights = capacitance_solve(terms, switch_susc)
     angles = solved_cols[:, 0, :] - jnp.einsum(
         "bit,it->bt", solved_cols[:, 1:, :], weights, precision=lax.Precision.HIGHEST

time: 244 us -> 236 us (0.967)
  blocking collectives: 19.6 us -> 13.1 us
    psum x1 -> x0, blocking collectives: 19.6 us -> none  [body(): terms = lax.psum(local_terms, 'front')]
    all_gather x0 -> x1, blocking collectives: none -> 13.1 us  [body(): terms = jnp.sum(lax.all_gather(local_terms, 'front'), axis=0)]
where the time goes in v1:
time: 236 us; the launch traced here: 235 us
  waiting for transfers between devices  117 us (50%)
  matrix products  34.9 us (15%)
  other arithmetic  32.3 us (14%)
  starting transfers between devices  25.1 us (11%)
  blocking collectives  13.1 us (6%)
  local copies, waits for them, and re-layouts  9.57 us (4%)
    ppermute x7, waiting for transfers between devices, from_behind(): return lax.ppermute(value, axis, pairs)  102 us
    dot_general x8, matrix products, product(): jnp.dot(operand, against, precision=lax.Precision.HIGHEST, preferred_elem...  29.7 us
    reduce_sum x32, other arithmetic, accumulate(): jnp.sum(centered_tanh(slot_block, in_weight, in_bias), axis=0)  23 us
    ppermute x7, starting transfers between devices, from_behind(): return lax.ppermute(value, axis, pairs)  21.6 us
    all_to_all x1, waiting for transfers between devices, body(): lax.all_to_all(outgoing, ('front', 'line'), split_axis=0, concat_axis=0,...  15.2 us
    all_gather x1, blocking collectives, body(): terms = jnp.sum(lax.all_gather(local_terms, 'front'), axis=0)  13.1 us
    sub x3, other arithmetic, upper_step(): return pivoted - arrived  6.33 us
  transfers between devices with their start and end apart: 8, of which 8 were waited for; matrix products, arithmetic and copies ran while one was open for 1% of the time, Pallas kernels for 0%

profile of v1, /device:TPU:0, one launch (start us, length us, event | category | flops | bytes accessed | tf_op | source)
XLA Modules:
  0.0 234.9 jit_solution(1498242732047019790)
XLA Ops:
  4.5 73.8 %while.32 = (s32[]{:T(128)}, f32[512,384]{1,0:T(8,128)}, f32[512,512]{1,0:T(8,128)S(1)}, f32[512,384]{1,0:T(8,128)S(1)}, s32[]{:T(128)}) while((s32[]{:T(128)}, f32[512,384]{1,0:T(8,128)}, f32[512,512]{1,0:T(8,128)S(1)}, f32[512,384]{1,0:T(8,128)S(1)}, s32[]{:T(128)}) %tuple.77), condition=%wide.region_4.0_spmd, body=%wide.region_3.0_spmd.sunk | while | flops 1208156160 | bytes 6553701 | solution.py:85
  4.5 5.8 %collective-permute-start = (f32[512,384]{1,0:T(8,128)}, f32[512,384]{1,0:T(8,128)}, u32[]{:S(2)}, u32[]{:S(2)}) collective-permute-start(f32[512,384]{1,0:T(8,128)} %get-tuple-element.285), channel_id=1, source_target_pairs={{0,4},{4,8},{8,12},{1,5},{5,9},{9,13},{2,6},{6,10},{10,14},{3,7},{... | collective-permute-start | bytes 2359304 | tf_op jit(solution)/shard_map/while/body/eval_jaxpr/ppermute | solution.py:13
  10.3 16.2 %collective-permute-done = f32[512,384]{1,0:T(8,128)} collective-permute-done((f32[512,384]{1,0:T(8,128)}, f32[512,384]{1,0:T(8,128)}, u32[]{:S(2)}, u32[]{:S(2)}) %collective-permute-start) | collective-permute-done | bytes 786464 | tf_op jit(solution)/shard_map/while/body/eval_jaxpr/ppermute | solution.py:13
  26.6 3.8 %convolution_subtract_fusion.2 = f32[512,384]{1,0:T(8,128)} fusion(f32[512,384]{1,0:T(8,128)S(1)} %get-tuple-element.292, f32[512,512]{1,0:T(8,128)S(1)} %get-tuple-element.291, f32[512,384]{1,0:T(8,128)} %collective-permute-done), kind=kOutput, calls=%fused_computation.2.clone.1 | convolution fusion | flops 1208156160 | bytes 3407872 | tf_op jit(solution)/shard_map/while/body/eval_jaxpr/dot_general | solution.py:17
  30.4 5.3 %collective-permute-start = (f32[512,384]{1,0:T(8,128)}, f32[512,384]{1,0:T(8,128)}, u32[]{:S(2)}, u32[]{:S(2)}) collective-permute-start(f32[512,384]{1,0:T(8,128)} %get-tuple-element.285), channel_id=1, source_target_pairs={{0,4},{4,8},{8,12},{1,5},{5,9},{9,13},{2,6},{6,10},{10,14},{3,7},{... | collective-permute-start | bytes 2359304 | tf_op jit(solution)/shard_map/while/body/eval_jaxpr/ppermute | solution.py:13
  35.7 15.3 %collective-permute-done = f32[512,384]{1,0:T(8,128)} collective-permute-done((f32[512,384]{1,0:T(8,128)}, f32[512,384]{1,0:T(8,128)}, u32[]{:S(2)}, u32[]{:S(2)}) %collective-permute-start) | collective-permute-done | bytes 786464 | tf_op jit(solution)/shard_map/while/body/eval_jaxpr/ppermute | solution.py:13
  51.0 3.8 %convolution_subtract_fusion.2 = f32[512,384]{1,0:T(8,128)} fusion(f32[512,384]{1,0:T(8,128)S(1)} %get-tuple-element.292, f32[512,512]{1,0:T(8,128)S(1)} %get-tuple-element.291, f32[512,384]{1,0:T(8,128)} %collective-permute-done), kind=kOutput, calls=%fused_computation.2.clone.1 | convolution fusion | flops 1208156160 | bytes 3407872 | tf_op jit(solution)/shard_map/while/body/eval_jaxpr/dot_general | solution.py:17
  54.8 5.3 %collective-permute-start = (f32[512,384]{1,0:T(8,128)}, f32[512,384]{1,0:T(8,128)}, u32[]{:S(2)}, u32[]{:S(2)}) collective-permute-start(f32[512,384]{1,0:T(8,128)} %get-tuple-element.285), channel_id=1, source_target_pairs={{0,4},{4,8},{8,12},{1,5},{5,9},{9,13},{2,6},{6,10},{10,14},{3,7},{... | collective-permute-start | bytes 2359304 | tf_op jit(solution)/shard_map/while/body/eval_jaxpr/ppermute | solution.py:13
  60.1 14.4 %collective-permute-done = f32[512,384]{1,0:T(8,128)} collective-permute-done((f32[512,384]{1,0:T(8,128)}, f32[512,384]{1,0:T(8,128)}, u32[]{:S(2)}, u32[]{:S(2)}) %collective-permute-start) | collective-permute-done | bytes 786464 | tf_op jit(solution)/shard_map/while/body/eval_jaxpr/ppermute | solution.py:13
  74.5 3.8 %convolution_subtract_fusion.2 = f32[512,384]{1,0:T(8,128)} fusion(f32[512,384]{1,0:T(8,128)S(1)} %get-tuple-element.292, f32[512,512]{1,0:T(8,128)S(1)} %get-tuple-element.291, f32[512,384]{1,0:T(8,128)} %collective-permute-done), kind=kOutput, calls=%fused_computation.2.clone.1 | convolution fusion | flops 1208156160 | bytes 3407872 | tf_op jit(solution)/shard_map/while/body/eval_jaxpr/dot_general | solution.py:17
  78.4 4.7 %convolution_bitcast_fusion = f32[512,384]{0,1:T(8,128)} fusion(f32[512,384]{1,0:T(8,128)} %get-tuple-element.98, f32[512,512]{1,0:T(8,128)S(1)} %copy-done), kind=kOutput, calls=%fused_computation.8 | convolution fusion | flops 1207959552 | bytes 2621440 | tf_op jit(solution)/shard_map/dot_general | solution.py:17
  83.0 1.4 copy.56
  85.3 72.7 %while.33 = (s32[]{:T(128)}, f32[512,384]{1,0:T(8,128)}, f32[512,512]{1,0:T(8,128)S(1)}, f32[512,384]{1,0:T(8,128)S(1)}, s32[]{:T(128)}) while((s32[]{:T(128)}, f32[512,384]{1,0:T(8,128)}, f32[512,512]{1,0:T(8,128)S(1)}, f32[512,384]{1,0:T(8,128)S(1)}, s32[]{:T(128)}) %tuple.78), condition=%wide.region_6.7_spmd, body=%wide.region_5.0_spmd.sunk | while | flops 1208156160 | bytes 8126565 | solution.py:92
  85.3 3.8 %fusion.40 = f32[512,384]{1,0:T(8,128)} fusion(f32[512,512]{1,0:T(8,128)S(1)} %get-tuple-element.306, f32[512,384]{1,0:T(8,128)} %get-tuple-element.300), kind=kOutput, calls=%fused_computation.57.clone.1 | convolution fusion | flops 1207959552 | bytes 2621440 | tf_op jit(solution)/shard_map/while/body/eval_jaxpr/dot_general | solution.py:17
  89.2 1.3 collective-permute-start.1
  90.5 18.2 %collective-permute-done.1 = f32[512,384]{1,0:T(8,128)} collective-permute-done((f32[512,384]{1,0:T(8,128)}, f32[512,384]{1,0:T(8,128)}, u32[]{:S(2)}, u32[]{:S(2)}) %collective-permute-start.1) | collective-permute-done | bytes 786464 | tf_op jit(solution)/shard_map/while/body/eval_jaxpr/ppermute | solution.py:13
  108.7 2.1 sub.95
  110.8 3.8 %fusion.40 = f32[512,384]{1,0:T(8,128)} fusion(f32[512,512]{1,0:T(8,128)S(1)} %get-tuple-element.306, f32[512,384]{1,0:T(8,128)} %get-tuple-element.300), kind=kOutput, calls=%fused_computation.57.clone.1 | convolution fusion | flops 1207959552 | bytes 2621440 | tf_op jit(solution)/shard_map/while/body/eval_jaxpr/dot_general | solution.py:17
  116.0 16.8 %collective-permute-done.1 = f32[512,384]{1,0:T(8,128)} collective-permute-done((f32[512,384]{1,0:T(8,128)}, f32[512,384]{1,0:T(8,128)}, u32[]{:S(2)}, u32[]{:S(2)}) %collective-permute-start.1) | collective-permute-done | bytes 786464 | tf_op jit(solution)/shard_map/while/body/eval_jaxpr/ppermute | solution.py:13
  132.8 2.1 sub.95
  134.9 3.8 %fusion.40 = f32[512,384]{1,0:T(8,128)} fusion(f32[512,512]{1,0:T(8,128)S(1)} %get-tuple-element.306, f32[512,384]{1,0:T(8,128)} %get-tuple-element.300), kind=kOutput, calls=%fused_computation.57.clone.1 | convolution fusion | flops 1207959552 | bytes 2621440 | tf_op jit(solution)/shard_map/while/body/eval_jaxpr/dot_general | solution.py:17
  140.0 15.9 %collective-permute-done.1 = f32[512,384]{1,0:T(8,128)} collective-permute-done((f32[512,384]{1,0:T(8,128)}, f32[512,384]{1,0:T(8,128)}, u32[]{:S(2)}, u32[]{:S(2)}) %collective-permute-start.1) | collective-permute-done | bytes 786464 | tf_op jit(solution)/shard_map/while/body/eval_jaxpr/ppermute | solution.py:13
  156.0 2.1 sub.95
  158.1 1.4 copy.58
  159.5 4.5 %convolution_bitcast_fusion.1 = f32[2,3,128]{1,0,2:T(2,128)S(1)} fusion(f32[512,3,128]{0,2,1:T(8,128)S(1)} %bitcast.102, f32[512,2,128]{0,2,1:T(8,128)S(1)} %convert_subtract_fusion), kind=kOutput, calls=%fused_computation.9 | convolution fusion | flops 4718592 | bytes 1313792 | tf_op jit(solution)/shard_map/bit,bct->ict/dot_general | solution.py:94
  164.1 13.1 %all-gather = f32[8,3,128]{2,1,0:T(4,128)S(1)} all-gather(f32[2,3,128]{2,1,0:T(4,128)S(1)} %copy.62), channel_id=2, replica_groups=mesh['groups'=2,'front'=4,'batch'=2,'line'=2] {'front'}, dimensions={0}, use_global_device_ids=true | all-gather | bytes 15360 | tf_op jit(solution)/shard_map/all_gather | solution.py:97
  177.8 1.5 collective-permute-start.2
  180.8 5.2 %collective-permute-done.2 = f32[512,128]{1,0:T(8,128)S(1)} collective-permute-done((f32[512,128]{1,0:T(8,128)S(1)}, f32[512,128]{1,0:T(8,128)S(1)}, u32[]{:S(2)}, u32[]{:S(2)}) %collective-permute-start.2) | collective-permute-done | bytes 262176 | tf_op jit(solution)/shard_map/ppermute | solution.py:13
  188.2 1.9 fusion
  190.1 3.5 %all-to-all-start = ((f32[8,128,128]{2,1,0:T(8,128)}), f32[8,128,128]{2,1,0:T(8,128)S(1)}, u32[]{:S(2)}, u32[]{:S(2)}) async-start(f32[8,128,128]{2,1,0:T(8,128)} %bitcast.14), calls=%async_computation | async-start | bytes 1048576 | tf_op jit(solution)/shard_map/all_to_all | solution.py:116
  193.7 15.2 %all-to-all-done = f32[8,128,128]{2,1,0:T(8,128)S(1)} async-done(((f32[8,128,128]{2,1,0:T(8,128)}), f32[8,128,128]{2,1,0:T(8,128)S(1)}, u32[]{:S(2)}, u32[]{:S(2)}) %all-to-all-start) | async-done | bytes 524320 | tf_op jit(solution)/shard_map/all_to_all | solution.py:116
  208.9 25.2 %while.34 = (s32[]{:T(128)}, f32[128,128]{1,0:T(8,128)S(1)}, f32[32,32,128]{2,1,0:T(8,128)S(1)}, f32[128]{0:T(128)S(1)}, f32[128]{0:T(128)S(1)}, /*index=5*/f32[1,1,128]{2,1,0:T(1,128)S(1)}, s32[]{:T(128)}, s32[]{:T(128)}) while((s32[]{:T(128)}, f32[128,128]{1,0:T(8,128)S(1)}, f32[32,32,128]{2,1,0:T(8,128)S(1)}, ...), condition=%wide.region_10.11_spmd.clone, body=%wide.region_8.10_spmd.clone.sunk | while | flops 2113539 | bytes 312931 | solution.py:125
  (153 shorter events, 36.1 us)
Async XLA Ops:
  0.6 77.7 %copy-start = (f32[512,512]{1,0:T(8,128)S(1)}, f32[512,512]{1,0:T(8,128)}, u32[]{:S(2)}) copy-start(f32[512,512]{1,0:T(8,128)} %param.24) | copy-start | bytes 3145732
  3.0 1.5 copy-start.1
  4.5 22.0 %collective-permute-start = (f32[512,384]{1,0:T(8,128)}, f32[512,384]{1,0:T(8,128)}, u32[]{:S(2)}, u32[]{:S(2)}) collective-permute-start(f32[512,384]{1,0:T(8,128)} %get-tuple-element.285), channel_id=1, source_target_pairs={{0,4},{4,8},{8,12},{1,5},{5,9},{9,13},{2,6},{6,10},{10,14},{3,7},{... | collective-permute-start | bytes 2359304 | tf_op jit(solution)/shard_map/while/body/eval_jaxpr/ppermute | solution.py:13
  30.4 20.6 %collective-permute-start = (f32[512,384]{1,0:T(8,128)}, f32[512,384]{1,0:T(8,128)}, u32[]{:S(2)}, u32[]{:S(2)}) collective-permute-start(f32[512,384]{1,0:T(8,128)} %get-tuple-element.285), channel_id=1, source_target_pairs={{0,4},{4,8},{8,12},{1,5},{5,9},{9,13},{2,6},{6,10},{10,14},{3,7},{... | collective-permute-start | bytes 2359304 | tf_op jit(solution)/shard_map/while/body/eval_jaxpr/ppermute | solution.py:13
  54.8 19.7 %collective-permute-start = (f32[512,384]{1,0:T(8,128)}, f32[512,384]{1,0:T(8,128)}, u32[]{:S(2)}, u32[]{:S(2)}) collective-permute-start(f32[512,384]{1,0:T(8,128)} %get-tuple-element.285), channel_id=1, source_target_pairs={{0,4},{4,8},{8,12},{1,5},{5,9},{9,13},{2,6},{6,10},{10,14},{3,7},{... | collective-permute-start | bytes 2359304 | tf_op jit(solution)/shard_map/while/body/eval_jaxpr/ppermute | solution.py:13
  89.2 19.5 %collective-permute-start.1 = (f32[512,384]{1,0:T(8,128)}, f32[512,384]{1,0:T(8,128)}, u32[]{:S(2)}, u32[]{:S(2)}) collective-permute-start(f32[512,384]{1,0:T(8,128)} %fusion.40), channel_id=1, source_target_pairs={{4,0},{8,4},{12,8},{5,1},{9,5},{13,9},{6,2},{10,6},{14,10},{7,3},{... | collective-permute-start | bytes 2359304 | tf_op jit(solution)/shard_map/while/body/eval_jaxpr/ppermute | solution.py:13
  114.7 18.1 %collective-permute-start.1 = (f32[512,384]{1,0:T(8,128)}, f32[512,384]{1,0:T(8,128)}, u32[]{:S(2)}, u32[]{:S(2)}) collective-permute-start(f32[512,384]{1,0:T(8,128)} %fusion.40), channel_id=1, source_target_pairs={{4,0},{8,4},{12,8},{5,1},{9,5},{13,9},{6,2},{10,6},{14,10},{7,3},{... | collective-permute-start | bytes 2359304 | tf_op jit(solution)/shard_map/while/body/eval_jaxpr/ppermute | solution.py:13
  138.8 17.2 %collective-permute-start.1 = (f32[512,384]{1,0:T(8,128)}, f32[512,384]{1,0:T(8,128)}, u32[]{:S(2)}, u32[]{:S(2)}) collective-permute-start(f32[512,384]{1,0:T(8,128)} %fusion.40), channel_id=1, source_target_pairs={{4,0},{8,4},{12,8},{5,1},{9,5},{13,9},{6,2},{10,6},{14,10},{7,3},{... | collective-permute-start | bytes 2359304 | tf_op jit(solution)/shard_map/while/body/eval_jaxpr/ppermute | solution.py:13
  159.5 17.8 %copy-start.8 = (f32[2,128]{1,0:T(2,128)S(1)}, f32[2,128]{1,0:T(2,128)}, u32[]{:S(2)}) copy-start(f32[2,128]{1,0:T(2,128)} %param.22) | copy-start | bytes 3076
  177.4 1.8 copy-start.6
  177.4 1.8 copy-start.7
  177.4 1.9 copy-start.4
  177.7 9.4 %copy-start.2 = (f32[512,128]{1,0:T(8,128)}, f32[512,128]{1,0:T(8,128)S(1)}, u32[]{:S(2)}) copy-start(f32[512,128]{1,0:T(8,128)S(1)} %bitcast_subtract_fusion) | copy-start | bytes 786436
  177.8 8.3 %collective-permute-start.2 = (f32[512,128]{1,0:T(8,128)S(1)}, f32[512,128]{1,0:T(8,128)S(1)}, u32[]{:S(2)}, u32[]{:S(2)}) collective-permute-start(f32[512,128]{1,0:T(8,128)S(1)} %bitcast_subtract_fusion), channel_id=1, source_target_pairs={{4,0},{8,4},{12,8},{5,1},{9,5},{13,9},{6,2},{10,6},{14,10},{7,3},{... | collective-permute-start | bytes 786440 | tf_op jit(solution)/shard_map/ppermute | solution.py:13
  187.1 1.1 copy-start.5
  188.2 5.5 %copy-start.10 = (f32[128]{0:T(128)S(1)}, f32[128]{0:T(128)}, u32[]{:S(2)}) copy-start(f32[128]{0:T(128)} %param.30) | copy-start | bytes 1540
  188.2 20.7 %copy-start.9 = (f32[128]{0:T(128)S(1)}, f32[128]{0:T(128)}, u32[]{:S(2)}) copy-start(f32[128]{0:T(128)} %param.29) | copy-start | bytes 1540
  190.1 18.8 %all-to-all-start = ((f32[8,128,128]{2,1,0:T(8,128)}), f32[8,128,128]{2,1,0:T(8,128)S(1)}, u32[]{:S(2)}, u32[]{:S(2)}) async-start(f32[8,128,128]{2,1,0:T(8,128)} %bitcast.14), calls=%async_computation | async-start | bytes 1048576 | tf_op jit(solution)/shard_map/all_to_all | solution.py:116
  208.9 25.2 %copy-start.3 = (bf16[128,128]{1,0:T(8,128)(2,1)S(1)}, bf16[128,128]{1,0:T(8,128)(2,1)}, u32[]{:S(2)}) copy-start(bf16[128,128]{1,0:T(8,128)(2,1)} %param.31) | copy-start | bytes 98308
